TPU v7x, 512 devices: a whole 4x8x8 slice. The times are simulated.
512 devices in a mesh: gx: 32 (over z_lo, y), gy: 16 (over z_hi, x, core).
Axes of the slice: x: 4, y: 8, z: 8 (z_hi: 2, z_lo: 4; z = z_hi * 4 + z_lo), core: 2. Of those that a mesh axis runs over, the one named last changes fastest.
Arguments:
- images: bfloat16 [262144, 1152], P(('gx', 'gy')), may hold values from -6 to 6
- texts: bfloat16 [262144, 1152], P(('gx', 'gy')), may hold values from -6 to 6
- log_scale: float32 [1], replicated, may hold values from 1.5 to 2.5
- bias: float32 [1], replicated, may hold values from -1 to 1
Outputs:
- image_grad: bfloat16 [262144, 1152], P(('gx', 'gy'))
- text_grad: bfloat16 [262144, 1152], P(('gx', 'gy'))
All inputs are finite; a program needn't handle non-finite values.
Results may differ from a plain program's by a relative error of at most 0.015.
Values may be sent and summed in bfloat16 or wider, within the bound.
A program may use at most 64 MiB of HBM per device.

v0:
```python
import jax
import jax.numpy as jnp
from jax import lax
from jax.sharding import PartitionSpec as P

STEPS = 2


def passed_along(block, axis, distance):
    devices = range(lax.axis_size(axis))
    route = [((i - distance) % len(devices), i) for i in devices]
    return lax.ppermute(block, axis, route)


def normalize(raw):
    values = raw.astype(jnp.float32)
    inverse = lax.rsqrt(jnp.sum(values * values, axis=-1, keepdims=True) + 1e-06)
    return (values * inverse, inverse)


def coefficient(image_block, text_block, shift_count, scale, offset):
    logits = (
        scale
        * lax.dot_general(
            image_block, text_block, (((1,), (1,)), ((), ())), preferred_element_type=jnp.float32
        )
        + offset
    )
    rows = image_block.shape[0]
    if shift_count == 0:
        same = lax.broadcasted_iota(jnp.int32, (rows, rows), 0) == lax.broadcasted_iota(
            jnp.int32, (rows, rows), 1
        )
        label = jnp.where(same, 1.0, -1.0).astype(jnp.float32)
    else:
        label = -jnp.ones((rows, rows), jnp.float32)
    grad = -label * jax.nn.sigmoid(-label * logits)
    return (scale * grad / (STEPS + 1)).astype(jnp.bfloat16)


def text_term(coef, image_low):
    return lax.dot_general(
        coef, image_low, (((0,), (0,)), ((), ())), preferred_element_type=jnp.float32
    )


def back_norm(unit, inverse, grad):
    return ((grad - unit * jnp.sum(unit * grad, axis=-1, keepdims=True)) * inverse).astype(
        jnp.bfloat16
    )


def on_device(images, texts, log_scale, bias):
    image_unit, image_inv = normalize(images)
    text_unit, text_inv = normalize(texts)
    image_low = image_unit.astype(jnp.bfloat16)
    text_low = text_unit.astype(jnp.bfloat16)
    scale = jnp.exp(log_scale[0])
    offset = bias[0]
    first = coefficient(image_low, text_low, 0, scale, offset)
    image_acc = jnp.dot(first, text_low, preferred_element_type=jnp.float32)
    text_acc = text_term(first, image_low)
    carried = text_low
    for shift_count in range(1, STEPS + 1):
        carried = passed_along(carried, ("gx", "gy"), 1)
        text_acc = passed_along(text_acc.astype(jnp.bfloat16), ("gx", "gy"), 1).astype(
            text_acc.dtype
        )
        coef = coefficient(image_low, carried, shift_count, scale, offset)
        image_acc = image_acc + jnp.dot(coef, carried, preferred_element_type=jnp.float32)
        text_acc = text_acc + text_term(coef, image_low)
    text_acc = passed_along(text_acc.astype(jnp.bfloat16), ("gx", "gy"), -STEPS).astype(
        text_acc.dtype
    )
    return (back_norm(image_unit, image_inv, image_acc), back_norm(text_unit, text_inv, text_acc))


def solution(mesh):
    return jax.shard_map(
        on_device,
        mesh=mesh,
        in_specs=(P(("gx", "gy"), None), P(("gx", "gy"), None), P(), P()),
        out_specs=(P(("gx", "gy"), None), P(("gx", "gy"), None)),
        check_vma=False,
    )
```

profile of v0, /device:TPU:128, one launch (start us, length us, event | category | flops | bytes accessed | tf_op | source)
XLA Modules:
  0.0 230.6 jit_solution(4801766389002554398)
XLA Ops:
  0.6 0.0 copy-start.1
  0.6 1.7 fusion.10
  2.3 0.0 copy-done.1
  2.3 0.0 copy-start
  2.3 0.3 fusion.1
  2.6 2.1 collective-permute-start
  4.7 0.0 copy-done
  4.7 0.3 fusion.9
  6.3 1.1 fusion.37
  7.5 0.9 convolution_convert_fusion
  8.4 3.5 %collective-permute-start.2 = (bf16[512,1152]{1,0:T(8,128)(2,1)S(1)}, bf16[512,1152]{1,0:T(8,128)(2,1)S(1)}, u32[]{:S(2)}, u32[]{:S(2)}) collective-permute-start(bf16[512,1152]{1,0:T(8,128)(2,1)S(1)} %convolution_convert_fusion), channel_id=1, source_target_pairs={{511,0},{0,1},{1,2},{2,3},{3,4},{4,5},{5,6},{6,7},{7,8},{8,9},{9,1... | collective-permute-start | bytes 3538952 | tf_op jit(solution)/shard_map/ppermute | solution.py:12
  11.9 44.2 %collective-permute-done = bf16[512,1152]{1,0:T(8,128)(2,1)S(1)} collective-permute-done((bf16[512,1152]{1,0:T(8,128)(2,1)S(1)}, bf16[512,1152]{1,0:T(8,128)(2,1)S(1)}, u32[]{:S(2)}, u32[]{:S(2)}) %collective-permute-start) | collective-permute-done | bytes 1179680 | tf_op jit(solution)/shard_map/ppermute | solution.py:12
  56.2 1.9 collective-permute-start.1
  58.1 1.1 fusion.38
  59.2 37.4 %collective-permute-done.2 = bf16[512,1152]{1,0:T(8,128)(2,1)S(1)} collective-permute-done((bf16[512,1152]{1,0:T(8,128)(2,1)S(1)}, bf16[512,1152]{1,0:T(8,128)(2,1)S(1)}, u32[]{:S(2)}, u32[]{:S(2)}) %collective-permute-start.2) | collective-permute-done | bytes 1179680 | tf_op jit(solution)/shard_map/ppermute | solution.py:12
  96.5 1.0 add_convert_fusion.1
  97.5 1.9 collective-permute-start.3
  99.4 0.9 fusion.50
  100.3 36.6 %collective-permute-done.1 = bf16[512,1152]{1,0:T(8,128)(2,1)S(1)} collective-permute-done((bf16[512,1152]{1,0:T(8,128)(2,1)S(1)}, bf16[512,1152]{1,0:T(8,128)(2,1)S(1)}, u32[]{:S(2)}, u32[]{:S(2)}) %collective-permute-start.1) | collective-permute-done | bytes 1179680 | tf_op jit(solution)/shard_map/ppermute | solution.py:12
  136.9 1.1 fusion.39
  137.9 0.9 fusion.40
  138.9 28.6 %collective-permute-done.3 = bf16[512,1152]{1,0:T(8,128)(2,1)S(1)} collective-permute-done((bf16[512,1152]{1,0:T(8,128)(2,1)S(1)}, bf16[512,1152]{1,0:T(8,128)(2,1)S(1)}, u32[]{:S(2)}, u32[]{:S(2)}) %collective-permute-start.3) | collective-permute-done | bytes 1179680 | tf_op jit(solution)/shard_map/ppermute | solution.py:12
  167.5 0.2 add_convert_fusion
  167.7 1.9 collective-permute-start.4
  169.6 0.8 convolution_add_fusion.1
  170.5 1.1 fusion.5
  171.6 1.5 fusion.8
  173.1 55.4 %collective-permute-done.4 = bf16[512,1152]{1,0:T(8,128)(2,1)S(1)} collective-permute-done((bf16[512,1152]{1,0:T(8,128)(2,1)S(1)}, bf16[512,1152]{1,0:T(8,128)(2,1)S(1)}, u32[]{:S(2)}, u32[]{:S(2)}) %collective-permute-start.4) | collective-permute-done | bytes 1179680 | tf_op jit(solution)/shard_map/ppermute | solution.py:12
  228.5 0.5 fusion.11
  229.0 1.6 fusion.13
  (2 shorter events, 0.0 us)
Async XLA Ops:
  0.6 1.7 copy-start.1
  2.3 2.3 %copy-start = (bf16[512,1152]{1,0:T(8,128)(2,1)S(1)}, bf16[512,1152]{1,0:T(8,128)(2,1)}, u32[]{:S(2)}) copy-start(bf16[512,1152]{1,0:T(8,128)(2,1)} %param.4) | copy-start | bytes 3538948
  2.6 53.6 %collective-permute-start = (bf16[512,1152]{1,0:T(8,128)(2,1)S(1)}, bf16[512,1152]{1,0:T(8,128)(2,1)S(1)}, u32[]{:S(2)}, u32[]{:S(2)}) collective-permute-start(bf16[512,1152]{1,0:T(8,128)(2,1)S(1)} %fusion.1), channel_id=1, source_target_pairs={{511,0},{0,1},{1,2},{2,3},{3,4},{4,5},{5,6},{6,7},{7,8},{8,9},{9,1... | collective-permute-start | bytes 3538952 | tf_op jit(solution)/shard_map/ppermute | solution.py:12
  8.4 88.1 %collective-permute-start.2 = (bf16[512,1152]{1,0:T(8,128)(2,1)S(1)}, bf16[512,1152]{1,0:T(8,128)(2,1)S(1)}, u32[]{:S(2)}, u32[]{:S(2)}) collective-permute-start(bf16[512,1152]{1,0:T(8,128)(2,1)S(1)} %convolution_convert_fusion), channel_id=1, source_target_pairs={{511,0},{0,1},{1,2},{2,3},{3,4},{4,5},{5,6},{6,7},{7,8},{8,9},{9,1... | collective-permute-start | bytes 3538952 | tf_op jit(solution)/shard_map/ppermute | solution.py:12
  56.2 80.7 %collective-permute-start.1 = (bf16[512,1152]{1,0:T(8,128)(2,1)S(1)}, bf16[512,1152]{1,0:T(8,128)(2,1)S(1)}, u32[]{:S(2)}, u32[]{:S(2)}) collective-permute-start(bf16[512,1152]{1,0:T(8,128)(2,1)S(1)} %collective-permute-done), channel_id=1, source_target_pairs={{511,0},{0,1},{1,2},{2,3},{3,4},{4,5},{5,6},{6,7},{7,8},{8,9},{9,1... | collective-permute-start | bytes 3538952 | tf_op jit(solution)/shard_map/ppermute | solution.py:12
  97.5 70.0 %collective-permute-start.3 = (bf16[512,1152]{1,0:T(8,128)(2,1)S(1)}, bf16[512,1152]{1,0:T(8,128)(2,1)S(1)}, u32[]{:S(2)}, u32[]{:S(2)}) collective-permute-start(bf16[512,1152]{1,0:T(8,128)(2,1)S(1)} %add_convert_fusion.1), channel_id=1, source_target_pairs={{511,0},{0,1},{1,2},{2,3},{3,4},{4,5},{5,6},{6,7},{7,8},{8,9},{9,1... | collective-permute-start | bytes 3538952 | tf_op jit(solution)/shard_map/ppermute | solution.py:12
  167.7 60.8 %collective-permute-start.4 = (bf16[512,1152]{1,0:T(8,128)(2,1)S(1)}, bf16[512,1152]{1,0:T(8,128)(2,1)S(1)}, u32[]{:S(2)}, u32[]{:S(2)}) collective-permute-start(bf16[512,1152]{1,0:T(8,128)(2,1)S(1)} %add_convert_fusion), channel_id=1, source_target_pairs={{2,0},{3,1},{4,2},{5,3},{6,4},{7,5},{8,6},{9,7},{10,8},{11,9},{12,... | collective-permute-start | bytes 3538952 | tf_op jit(solution)/shard_map/ppermute | solution.py:12
where the time goes:
time: 231 us
  waiting for transfers between devices  202 us (87%)
  starting transfers between devices  11.3 us (5%)
  matrix products  8.95 us (4%)
  other arithmetic  6.09 us (3%)
    ppermute x5, waiting for transfers between devices, passed_along(): return lax.ppermute(block, axis, route)  202 us
    ppermute x5, starting transfers between devices, passed_along(): return lax.ppermute(block, axis, route)  11.3 us
  transfers between devices with their start and end apart: 5, of which 5 were waited for; matrix products, arithmetic and copies ran while one was open for 5% of the time, Pallas kernels for 0%

commit v1 on v0

v1 whole, which is shorter than its diff:
```python
import functools

import jax
import jax.numpy as jnp
from jax import lax
from jax.experimental import pallas as pl
from jax.experimental.pallas import tpu as pltpu
from jax.sharding import PartitionSpec as P

STEPS = 2
MESH = pl.DeviceIdType.MESH
CHUNK = 128
RELAYED = 0


def kernel(
    n, scale_ref, bias_ref, images_ref, texts_ref, image_out, text_out,
    raw, low, inverse, total, far, near, relay, result,
    load_sem, store_sem, far_send, far_recv, near_send, near_recv, pass_send, pass_recv,
):
    rows, width = raw.shape[1:]
    chunks = rows // CHUNK
    gx, gy = lax.axis_index("gx"), lax.axis_index("gy")
    inner = lax.axis_size("gy")
    me = gx * inner + gy
    core = lax.rem(gy, 2)
    x = lax.rem(gy // 2, 4)

    def at(distance):
        there = lax.rem(me + distance + n, n)
        return (there // inner, lax.rem(there, inner))

    sibling = (gx, gy + 1 - 2 * core)
    after, before = at(2), at(-2)

    barrier = pltpu.get_barrier_semaphore()
    for partner in (after, before, sibling):
        pl.semaphore_signal(barrier, inc=1, device_id=partner, device_id_type=MESH)

    loads = [
        pltpu.make_async_copy(ref, raw.at[side], load_sem.at[side])
        for side, ref in enumerate((images_ref, texts_ref))
    ]
    for load in loads:
        load.start()
    for side in range(2):
        loads[side].wait()

        @pl.loop(0, chunks)
        def _(j):
            span = pl.ds(j * CHUNK, CHUNK)
            values = raw[side, span, :].astype(jnp.float32)
            inv = lax.rsqrt(jnp.sum(values * values, axis=-1, keepdims=True) + 1e-06)
            inverse[side, span, :] = inv
            low[side, span, :] = (values * inv).astype(jnp.bfloat16)

    pl.semaphore_wait(barrier, 3)

    def far_copy(side, j, partner):
        span = pl.ds(j * CHUNK, CHUNK)
        return pltpu.make_async_remote_copy(
            src_ref=low.at[1 - side, span],
            dst_ref=far.at[side, span],
            send_sem=far_send.at[side, j],
            recv_sem=far_recv.at[side, j],
            device_id=partner,
            device_id_type=MESH,
        )

    def near_copy(source, side, j):
        span = pl.ds(j * CHUNK, CHUNK)
        return pltpu.make_async_remote_copy(
            src_ref=source.at[span],
            dst_ref=near.at[side, span],
            send_sem=near_send.at[side, j],
            recv_sem=near_recv.at[side, j],
            device_id=sibling,
            device_id_type=MESH,
        )

    @pl.loop(0, chunks)
    def _(j):
        far_copy(0, j, after).start()
        far_copy(1, j, before).start()

    @pl.loop(0, chunks)
    def _(j):
        near_copy(low.at[1 - core], core, j).start()

    scale = jnp.exp(jnp.full((1, CHUNK), scale_ref[0], jnp.float32))
    offset = bias_ref[0]
    third = scale / (STEPS + 1)

    def weigh(side, other, j, own):
        logits = scale * lax.dot_general(
            low[side], other, (((1,), (1,)), ((), ())), preferred_element_type=jnp.float32
        ) + offset
        if own:
            same = lax.broadcasted_iota(jnp.int32, logits.shape, 0) == j * CHUNK + (
                lax.broadcasted_iota(jnp.int32, logits.shape, 1)
            )
            part = jax.nn.sigmoid(jnp.where(same, -logits, logits))
            coef = (jnp.where(same, -part, part) * third).astype(jnp.bfloat16)
        else:
            coef = (jax.nn.sigmoid(logits) * third).astype(jnp.bfloat16)
        return jnp.dot(coef, other, preferred_element_type=jnp.float32)

    for side in range(2):

        @pl.loop(0, chunks)
        def _(j):
            part = weigh(side, low[1 - side, pl.ds(j * CHUNK, CHUNK), :], j, True)

            @pl.when(j == 0)
            def _():
                total[side] = part

            @pl.when(j > 0)
            def _():
                total[side] += part

    def add_near(side, j):
        near_copy(low.at[0], side, j).wait_recv()
        total[side] += weigh(side, near[side, pl.ds(j * CHUNK, CHUNK), :], j, False)

    @pl.loop(0, chunks)
    def _(j):
        add_near(1 - core, j)

    @pl.loop(0, chunks)
    def _(j):
        for side in range(2):
            far_copy(side, j, after).wait_recv()

            @pl.when(core == 1 - side)
            def _():
                near_copy(far.at[side], side, j).start()

            total[side] += weigh(side, far[side, pl.ds(j * CHUNK, CHUNK), :], j, False)
        add_near(core, j)

    for side, out in enumerate((image_out, text_out)):

        @pl.loop(0, chunks)
        def _(j):
            span = pl.ds(j * CHUNK, CHUNK)
            inv = inverse[side, span, :]
            unit = raw[side, span, :].astype(jnp.float32) * inv
            grad = total[side, span, :]
            along = jnp.sum(unit * grad, axis=-1, keepdims=True)
            result[side, span, :] = ((grad - unit * along) * inv).astype(jnp.bfloat16)

        pltpu.make_async_copy(result.at[side], out, store_sem.at[side]).start()

    @pl.loop(0, chunks)
    def _(j):
        for side in range(2):
            far_copy(side, j, after).wait_send()
            near_copy(low.at[0], side, j).wait_send()

    for side, out in enumerate((image_out, text_out)):
        pltpu.make_async_copy(result.at[side], out, store_sem.at[side]).wait()


def on_device(images, texts, log_scale, bias):
    rows, width = images.shape
    chunks = rows // CHUNK
    n = lax.axis_size("gx") * lax.axis_size("gy")
    block = (2, rows, width)
    dma = pltpu.SemaphoreType.DMA
    return pl.pallas_call(
        functools.partial(kernel, n),
        out_shape=[jax.ShapeDtypeStruct((rows, width), jnp.bfloat16)] * 2,
        in_specs=[pl.BlockSpec(memory_space=pltpu.SMEM)] * 2 + [pl.BlockSpec(memory_space=pl.ANY)] * 2,
        out_specs=[pl.BlockSpec(memory_space=pl.ANY)] * 2,
        scratch_shapes=[
            pltpu.VMEM(block, jnp.bfloat16),
            pltpu.VMEM(block, jnp.bfloat16),
            pltpu.VMEM((2, rows, 1), jnp.float32),
            pltpu.VMEM(block, jnp.float32),
            pltpu.VMEM(block, jnp.bfloat16),
            pltpu.VMEM(block, jnp.bfloat16),
            pltpu.VMEM((rows, width), jnp.bfloat16),
            pltpu.VMEM(block, jnp.bfloat16),
            dma((2,)),
            dma((2,)),
            dma((2, chunks)),
            dma((2, chunks)),
            dma((2, chunks)),
            dma((2, chunks)),
            dma((chunks,)),
            dma((chunks,)),
        ],
        compiler_params=pltpu.CompilerParams(
            collective_id=0, has_side_effects=True, vmem_limit_bytes=48 * 1024 * 1024
        ),
        cost_estimate=pl.CostEstimate(
            flops=24 * rows * rows * width, bytes_accessed=8 * rows * width, transcendentals=6 * rows * rows
        ),
        name="contrast",
    )(log_scale, bias, images, texts)


def solution(mesh):
    return jax.shard_map(
        on_device,
        mesh=mesh,
        in_specs=(P(("gx", "gy"), None), P(("gx", "gy"), None), P(), P()),
        out_specs=(P(("gx", "gy"), None), P(("gx", "gy"), None)),
        check_vma=False,
    )
```

time: 231 us -> 103 us (0.45)
  waiting for transfers between devices: 202 us -> 0 us
  Pallas kernels: 0 us -> 95.9 us
  starting transfers between devices: 11.3 us -> 0 us
  matrix products: 8.95 us -> 0 us
  other arithmetic: 6.09 us -> 0 us
  local copies, waits for them, and re-layouts: 0.01 us -> 4.56 us
    ppermute x5 -> x0, waiting for transfers between devices: 202 us -> none  [passed_along(): return lax.ppermute(block, axis, route)]
    pallas_call x0 -> x1, Pallas kernels: none -> 95.9 us  [on_device(): pl.pallas_call(functools.partial(kernel, n), out_shape=[jax.ShapeDtypeStr...]
    ppermute x5 -> x0, starting transfers between devices: 11.3 us -> none  [passed_along(): return lax.ppermute(block, axis, route)]
    dot_general x9 -> x0, matrix products: 8.95 us -> none  [the longest x3 3.26 us: coefficient(): lax.dot_general(image_block, text_block, (((1,), (1,)), ((), ())), prefer...]
    unnamed x4 -> x6, local copies, waits for them, and re-layouts: 0.01 us -> 4.56 us
    convert_element_type x4 -> x0, other arithmetic: 3.58 us -> none  [the longest x2 3.11 us: back_norm(): ((grad - unit * jnp.sum(unit * grad, axis=-1, keepdims=True)) * inverse)....]
    reduce_sum x3 -> x0, other arithmetic: 2.5 us -> none  [the longest x2 1.98 us: normalize(): jnp.sum(values * values, axis=-1, keepdims=True) + 1e-06]
  transfers between devices with their start and end apart: 5 -> 0, of which waited for: 5 -> 0; matrix products, arithmetic and copies ran while one was open for 5% -> 0% of each run, Pallas kernels for 0% -> 0%
where the time goes in v1:
time: 103 us; the launch traced here: 102 us
  Pallas kernels  95.9 us (93%)
  local copies, waits for them, and re-layouts  4.56 us (4%)
  between operations  1.94 us (2%)
    pallas_call x1, Pallas kernels, on_device(): pl.pallas_call(functools.partial(kernel, n), out_shape=[jax.ShapeDtypeStr...  95.9 us
    unnamed x6, local copies, waits for them, and re-layouts  4.56 us

profile of v1, /device:TPU:128, one launch (start us, length us, event | category | flops | bytes accessed | tf_op | source)
XLA Modules:
  0.0 102.4 jit_solution(16569156396508941996)
XLA Ops:
  1.9 0.0 copy-start
  1.9 1.3 %copy-done = bf16[512,1152]{1,0:T(8,128)(2,1)S(1)} copy-done((bf16[512,1152]{1,0:T(8,128)(2,1)S(1)}, bf16[512,1152]{1,0:T(8,128)(2,1)}, u32[]{:S(2)}) %copy-start) | copy-done | bytes 1179672
  3.2 0.0 copy-start.1
  3.2 1.3 %copy-done.1 = bf16[512,1152]{1,0:T(8,128)(2,1)S(1)} copy-done((bf16[512,1152]{1,0:T(8,128)(2,1)S(1)}, bf16[512,1152]{1,0:T(8,128)(2,1)}, u32[]{:S(2)}) %copy-start.1) | copy-done | bytes 1179672
  4.5 95.9 %contrast.1 = (bf16[512,1152]{1,0:T(8,128)(2,1)S(1)}, bf16[512,1152]{1,0:T(8,128)(2,1)S(1)}) custom-call(f32[1]{0:T(128)S(6)} %copy.8.scale_ref, f32[1]{0:T(128)S(6)} %copy.9.bias_ref, bf16[512,1152]{1,0:T(8,128)(2,1)S(1)} %copy-done, bf16[512,1152]{1,0:T(8,128)(2,1)S(1)} %copy-done.1), custom_call_target="tpu_custom_call" | custom-call | flops 7247757312 | bytes 4718592 | tf_op jit(solution)/shard_map/contrast/pallas_call | solution.py:171
  100.3 1.0 copy.10
  101.3 1.0 copy.11
Async XLA Ops:
  1.9 1.3 %copy-start = (bf16[512,1152]{1,0:T(8,128)(2,1)S(1)}, bf16[512,1152]{1,0:T(8,128)(2,1)}, u32[]{:S(2)}) copy-start(bf16[512,1152]{1,0:T(8,128)(2,1)} %images_ref.1) | copy-start | bytes 3538948
  3.2 1.3 %copy-start.1 = (bf16[512,1152]{1,0:T(8,128)(2,1)S(1)}, bf16[512,1152]{1,0:T(8,128)(2,1)}, u32[]{:S(2)}) copy-start(bf16[512,1152]{1,0:T(8,128)(2,1)} %texts_ref.1) | copy-start | bytes 3538948

commit v2 on v1

--- a/solution.py
+++ b/solution.py
@@ -9,8 +9,10 @@
 
 STEPS = 2
 MESH = pl.DeviceIdType.MESH
-CHUNK = 128
-RELAYED = 0
+CHUNK = 256
+PIECES = 8
+GROUP = 4
+RELAYED = 2
 
 
 def kernel(
@@ -56,8 +58,15 @@
 
     pl.semaphore_wait(barrier, 3)
 
+    size = rows // PIECES
+    edge = jnp.logical_or(x == 0, x == 3)
+    middle = jnp.logical_not(edge)
+    passing = jnp.where(x >= 2, 0, 1)
+    inward = at(jnp.where(x == 3, -2, 2))
+    onward = at(jnp.where(x == 2, 4, -4))
+
     def far_copy(side, j, partner):
-        span = pl.ds(j * CHUNK, CHUNK)
+        span = pl.ds(j * size, size)
         return pltpu.make_async_remote_copy(
             src_ref=low.at[1 - side, span],
             dst_ref=far.at[side, span],
@@ -67,8 +76,30 @@
             device_id_type=MESH,
         )
 
+    def relay_copy(j):
+        span = pl.ds(j * size, size)
+        return pltpu.make_async_remote_copy(
+            src_ref=low.at[1 - passing, span],
+            dst_ref=relay.at[span],
+            send_sem=far_send.at[passing, j],
+            recv_sem=pass_recv.at[j],
+            device_id=inward,
+            device_id_type=MESH,
+        )
+
+    def onward_copy(j):
+        span = pl.ds(j * size, size)
+        return pltpu.make_async_remote_copy(
+            src_ref=relay.at[span],
+            dst_ref=far.at[passing, span],
+            send_sem=pass_send.at[j],
+            recv_sem=far_recv.at[passing, j],
+            device_id=onward,
+            device_id_type=MESH,
+        )
+
     def near_copy(source, side, j):
-        span = pl.ds(j * CHUNK, CHUNK)
+        span = pl.ds(j * size, size)
         return pltpu.make_async_remote_copy(
             src_ref=source.at[span],
             dst_ref=near.at[side, span],
@@ -78,14 +109,34 @@
             device_id_type=MESH,
         )
 
-    @pl.loop(0, chunks)
-    def _(j):
-        far_copy(0, j, after).start()
-        far_copy(1, j, before).start()
-
-    @pl.loop(0, chunks)
+    def relayed(j):
+        return lax.rem(j, GROUP) < RELAYED
+
+    @pl.loop(0, PIECES)
+    def _(j):
+        @pl.when(jnp.logical_and(edge, relayed(j)))
+        def _():
+            relay_copy(j).start()
+
+    @pl.loop(0, PIECES)
+    def _(j):
+        for side, partner in enumerate((after, before)):
+            through = jnp.logical_and(x == 3 - 3 * side, relayed(j))
+
+            @pl.when(jnp.logical_not(through))
+            def _():
+                far_copy(side, j, partner).start()
+
+    @pl.loop(0, PIECES)
     def _(j):
         near_copy(low.at[1 - core], core, j).start()
+
+    @pl.loop(0, PIECES)
+    def _(j):
+        @pl.when(jnp.logical_and(middle, relayed(j)))
+        def _():
+            relay_copy(j).wait_recv()
+            onward_copy(j).start()
 
     scale = jnp.exp(jnp.full((1, CHUNK), scale_ref[0], jnp.float32))
     offset = bias_ref[0]
@@ -120,7 +171,8 @@
                 total[side] += part
 
     def add_near(side, j):
-        near_copy(low.at[0], side, j).wait_recv()
+        for i in range(GROUP):
+            near_copy(low.at[0], side, j * GROUP + i).wait_recv()
         total[side] += weigh(side, near[side, pl.ds(j * CHUNK, CHUNK), :], j, False)
 
     @pl.loop(0, chunks)
@@ -130,11 +182,12 @@
     @pl.loop(0, chunks)
     def _(j):
         for side in range(2):
-            far_copy(side, j, after).wait_recv()
-
-            @pl.when(core == 1 - side)
-            def _():
-                near_copy(far.at[side], side, j).start()
+            for i in range(GROUP):
+                far_copy(side, j * GROUP + i, after).wait_recv()
+
+                @pl.when(core == 1 - side)
+                def _():
+                    near_copy(far.at[side], side, j * GROUP + i).start()
 
             total[side] += weigh(side, far[side, pl.ds(j * CHUNK, CHUNK), :], j, False)
         add_near(core, j)
@@ -152,19 +205,22 @@
 
         pltpu.make_async_copy(result.at[side], out, store_sem.at[side]).start()
 
-    @pl.loop(0, chunks)
+    @pl.loop(0, PIECES)
     def _(j):
         for side in range(2):
             far_copy(side, j, after).wait_send()
             near_copy(low.at[0], side, j).wait_send()
 
+        @pl.when(jnp.logical_and(middle, relayed(j)))
+        def _():
+            onward_copy(j).wait_send()
+
     for side, out in enumerate((image_out, text_out)):
         pltpu.make_async_copy(result.at[side], out, store_sem.at[side]).wait()
 
 
 def on_device(images, texts, log_scale, bias):
     rows, width = images.shape
-    chunks = rows // CHUNK
     n = lax.axis_size("gx") * lax.axis_size("gy")
     block = (2, rows, width)
     dma = pltpu.SemaphoreType.DMA
@@ -184,12 +240,12 @@
             pltpu.VMEM(block, jnp.bfloat16),
             dma((2,)),
             dma((2,)),
-            dma((2, chunks)),
-            dma((2, chunks)),
-            dma((2, chunks)),
-            dma((2, chunks)),
-            dma((chunks,)),
-            dma((chunks,)),
+            dma((2, PIECES)),
+            dma((2, PIECES)),
+            dma((2, PIECES)),
+            dma((2, PIECES)),
+            dma((PIECES,)),
+            dma((PIECES,)),
         ],
         compiler_params=pltpu.CompilerParams(
             collective_id=0, has_side_effects=True, vmem_limit_bytes=48 * 1024 * 1024

time: 103 us -> 70.7 us (0.69)
  Pallas kernels: 95.9 us -> 63.4 us
    pallas_call x1, Pallas kernels: 95.9 us -> 63.4 us  [on_device(): pl.pallas_call(functools.partial(kernel, n), out_shape=[jax.ShapeDtypeStr...]
where the time goes in v2:
time: 70.7 us; the launch traced here: 69.9 us
  Pallas kernels  63.4 us (90%)
  local copies, waits for them, and re-layouts  4.56 us (6%)
  between operations  1.94 us (3%)
    pallas_call x1, Pallas kernels, on_device(): pl.pallas_call(functools.partial(kernel, n), out_shape=[jax.ShapeDtypeStr...  63.4 us
    unnamed x6, local copies, waits for them, and re-layouts  4.56 us

profile of v2, /device:TPU:128, one launch (start us, length us, event | category | flops | bytes accessed | tf_op | source)
XLA Modules:
  0.0 69.9 jit_solution(17503382817285088291)
XLA Ops:
  1.9 0.0 copy-start
  1.9 1.3 %copy-done = bf16[512,1152]{1,0:T(8,128)(2,1)S(1)} copy-done((bf16[512,1152]{1,0:T(8,128)(2,1)S(1)}, bf16[512,1152]{1,0:T(8,128)(2,1)}, u32[]{:S(2)}) %copy-start) | copy-done | bytes 1179672
  3.2 0.0 copy-start.1
  3.2 1.3 %copy-done.1 = bf16[512,1152]{1,0:T(8,128)(2,1)S(1)} copy-done((bf16[512,1152]{1,0:T(8,128)(2,1)S(1)}, bf16[512,1152]{1,0:T(8,128)(2,1)}, u32[]{:S(2)}) %copy-start.1) | copy-done | bytes 1179672
  4.5 63.4 %contrast.1 = (bf16[512,1152]{1,0:T(8,128)(2,1)S(1)}, bf16[512,1152]{1,0:T(8,128)(2,1)S(1)}) custom-call(f32[1]{0:T(128)S(6)} %copy.8.scale_ref, f32[1]{0:T(128)S(6)} %copy.9.bias_ref, bf16[512,1152]{1,0:T(8,128)(2,1)S(1)} %copy-done, bf16[512,1152]{1,0:T(8,128)(2,1)S(1)} %copy-done.1), custom_call_target="tpu_custom_call" | custom-call | flops 7247757312 | bytes 4718592 | tf_op jit(solution)/shard_map/contrast/pallas_call | solution.py:227
  67.8 1.0 %copy.10 = bf16[512,1152]{1,0:T(8,128)(2,1)} copy(bf16[512,1152]{1,0:T(8,128)(2,1)S(1)} %get-tuple-element.4) | data formatting | bytes 2359296
  68.9 1.0 %copy.11 = bf16[512,1152]{1,0:T(8,128)(2,1)} copy(bf16[512,1152]{1,0:T(8,128)(2,1)S(1)} %get-tuple-element.5) | data formatting | bytes 2359296
Async XLA Ops:
  1.9 1.3 %copy-start = (bf16[512,1152]{1,0:T(8,128)(2,1)S(1)}, bf16[512,1152]{1,0:T(8,128)(2,1)}, u32[]{:S(2)}) copy-start(bf16[512,1152]{1,0:T(8,128)(2,1)} %images_ref.1) | copy-start | bytes 3538948
  3.2 1.3 %copy-start.1 = (bf16[512,1152]{1,0:T(8,128)(2,1)S(1)}, bf16[512,1152]{1,0:T(8,128)(2,1)}, u32[]{:S(2)}) copy-start(bf16[512,1152]{1,0:T(8,128)(2,1)} %texts_ref.1) | copy-start | bytes 3538948

commit v3 on v2

v3 whole, which is shorter than its diff:
```python
import functools

import jax
import jax.numpy as jnp
from jax import lax
from jax.experimental import pallas as pl
from jax.experimental.pallas import tpu as pltpu
from jax.sharding import PartitionSpec as P

STEPS = 2
MESH = pl.DeviceIdType.MESH
PIECES = 8
GROUP = 4
RELAYED = 2
AHEAD = 4


def kernel(
    n, scale_ref, bias_ref, images_ref, texts_ref, image_out, text_out,
    raw, low, inverse, total, far, near, relay, bend,
    load_sem, far_send, far_recv, near_send, near_recv, pass_send, pass_recv,
    bend_send, bend_recv, go_sem,
):
    rows, width = raw.shape[1:]
    size = rows // PIECES
    chunk = size * GROUP
    gx, gy = lax.axis_index("gx"), lax.axis_index("gy")
    inner = lax.axis_size("gy")
    me = gx * inner + gy
    core = lax.rem(gy, 2)
    x = lax.rem(gy // 2, 4)
    edge = jnp.logical_or(x == 0, x == 3)
    middle = jnp.logical_not(edge)
    early = gy < inner // 2
    waits = jnp.logical_and(edge, early)
    opens = jnp.logical_and(edge, jnp.logical_not(early))

    def at(distance):
        there = lax.rem(me + distance + n, n)
        return (there // inner, lax.rem(there, inner))

    sibling = (gx, gy + 1 - 2 * core)
    after, before = at(2), at(-2)
    across = at(jnp.where(x == 3, 2, -2))
    helper = at(jnp.where(x == 3, -4, 4))
    helped = at(jnp.where(x == 1, 4, -4))
    onward = at(jnp.where(x == 1, 6, -6))
    passing = 1 - lax.rem(x, 2)

    y, z = lax.rem(gx, 8), gx // 8 + 4 * (gy // 8)
    forth, back = passing == 0, passing == 1
    bent = jnp.logical_or(
        jnp.logical_and(forth, jnp.logical_and(y == 7, z == 5)),
        jnp.logical_and(back, jnp.logical_and(y == 0, z == 2)),
    )
    bends = jnp.logical_and(z == 0, y == 7 * passing)
    corner = (7 * passing, lax.rem(gy, 8))
    bent_from = (jnp.where(forth, 15, 16), jnp.where(forth, lax.rem(gy, 8) + 8, lax.rem(gy, 8)))
    bent_to = (jnp.where(forth, 16, 15), jnp.where(forth, core, 14 + core))

    barrier = pltpu.get_barrier_semaphore()
    pl.semaphore_signal(barrier, inc=1, device_id=sibling, device_id_type=MESH)
    for partner, last in ((after, 3), (before, 0)):

        @pl.when(jnp.logical_not(jnp.logical_and(opens, x == last)))
        def _():
            pl.semaphore_signal(barrier, inc=1, device_id=partner, device_id_type=MESH)

    @pl.when(middle)
    def _():
        pl.semaphore_signal(barrier, inc=1, device_id=helped, device_id_type=MESH)

    @pl.when(bends)
    def _():
        pl.semaphore_signal(barrier, inc=1, device_id=bent_from, device_id_type=MESH)

    greetings = 3 + edge.astype(jnp.int32) - waits.astype(jnp.int32) + bent.astype(jnp.int32)

    def load(ref, index, g):
        span = pl.ds(g * chunk, chunk)
        return pltpu.make_async_copy(ref.at[span], raw.at[index, span], load_sem.at[index, g])

    first = jnp.where(opens, 1 - passing, passing)
    for turn in range(2):
        for index, ref in enumerate((images_ref, texts_ref)):

            @pl.when(index == (first if turn == 0 else 1 - first))
            def _():
                for g in range(rows // chunk):
                    load(ref, index, g).start()

    def wait_load(index, j):
        @pl.when(lax.rem(j, GROUP) == 0)
        def _():
            load(images_ref, index, j // GROUP).wait()

    def far_copy(side, j, partner):
        span = pl.ds(j * size, size)
        return pltpu.make_async_remote_copy(
            src_ref=low.at[1 - side, span],
            dst_ref=far.at[side, span],
            send_sem=far_send.at[side, j],
            recv_sem=far_recv.at[side, j],
            device_id=partner,
            device_id_type=MESH,
        )

    def relay_copy(j):
        span = pl.ds(j * size, size)
        return pltpu.make_async_remote_copy(
            src_ref=low.at[1 - passing, span],
            dst_ref=relay.at[span],
            send_sem=far_send.at[passing, j],
            recv_sem=pass_recv.at[j],
            device_id=helper,
            device_id_type=MESH,
        )

    def onward_copy(j):
        span = pl.ds(j * size, size)
        return pltpu.make_async_remote_copy(
            src_ref=relay.at[span],
            dst_ref=far.at[passing, span],
            send_sem=pass_send.at[j],
            recv_sem=far_recv.at[passing, j],
            device_id=onward,
            device_id_type=MESH,
        )

    def bent_copy(source, send_sem, j):
        span = pl.ds(j * size, size)
        return pltpu.make_async_remote_copy(
            src_ref=source.at[span],
            dst_ref=bend.at[span],
            send_sem=send_sem,
            recv_sem=bend_recv.at[j],
            device_id=corner,
            device_id_type=MESH,
        )

    def last_copy(j):
        span = pl.ds(j * size, size)
        return pltpu.make_async_remote_copy(
            src_ref=bend.at[span],
            dst_ref=far.at[passing, span],
            send_sem=bend_send.at[j],
            recv_sem=far_recv.at[passing, j],
            device_id=bent_to,
            device_id_type=MESH,
        )

    def near_copy(source, side, j):
        span = pl.ds(j * size, size)
        return pltpu.make_async_remote_copy(
            src_ref=source.at[span],
            dst_ref=near.at[side, span],
            send_sem=near_send.at[side, j],
            recv_sem=near_recv.at[side, j],
            device_id=sibling,
            device_id_type=MESH,
        )

    def relayed(j):
        return lax.rem(j, GROUP) < RELAYED

    def send_across(j):
        @pl.when(relayed(j))
        def _():
            relay_copy(j).start()

        straight = jnp.logical_not(relayed(j))

        @pl.when(jnp.logical_and(straight, jnp.logical_not(bent)))
        def _():
            far_copy(passing, j, across).start()

        @pl.when(jnp.logical_and(straight, bent))
        def _():
            bent_copy(low.at[1 - passing], far_send.at[passing, j], j).start()

    def bent_here(j):
        return jnp.logical_and(bends, relayed(j) == middle)

    def normalize(index, j):
        span = pl.ds(j * size, size)
        values = raw[index, span, :].astype(jnp.float32)
        inv = lax.rsqrt(jnp.sum(values * values, axis=-1, keepdims=True) + 1e-06)
        inverse[index, span, :] = inv
        low[index, span, :] = (values * inv).astype(jnp.bfloat16)

    def send_along(side, j):
        for fixed, partner in enumerate((after, before)):

            @pl.when(side == fixed)
            def _():
                far_copy(fixed, j, partner).start()

    def enter(j):
        @pl.when(j == 0)
        def _():
            pl.semaphore_wait(barrier, greetings)

            @pl.when(opens)
            def _():
                pl.semaphore_signal(go_sem, inc=1, device_id=across, device_id_type=MESH)

    @pl.loop(0, PIECES)
    def _(j):
        wait_load(first, j)
        normalize(first, j)
        enter(j)

        @pl.when(opens)
        def _():
            send_across(j)

        @pl.when(jnp.logical_or(middle, jnp.logical_and(waits, j < AHEAD)))
        def _():
            send_along(1 - first, j)

    @pl.loop(0, PIECES)
    def _(j):
        wait_load(1 - first, j)
        normalize(1 - first, j)

        @pl.when(jnp.logical_or(middle, opens))
        def _():
            send_along(first, j)

        near_copy(low.at[1 - core], core, j).start()

    scale = jnp.exp(jnp.full((1, chunk), scale_ref[0], jnp.float32))
    offset = bias_ref[0]
    third = scale / (STEPS + 1)

    def weigh(side, other, j, own):
        logits = scale * lax.dot_general(
            low[side], other, (((1,), (1,)), ((), ())), preferred_element_type=jnp.float32
        ) + offset
        if own:
            same = lax.broadcasted_iota(jnp.int32, logits.shape, 0) == j * chunk + (
                lax.broadcasted_iota(jnp.int32, logits.shape, 1)
            )
            part = jax.nn.sigmoid(jnp.where(same, -logits, logits))
            coef = (jnp.where(same, -part, part) * third).astype(jnp.bfloat16)
        else:
            coef = (jax.nn.sigmoid(logits) * third).astype(jnp.bfloat16)
        return jnp.dot(coef, other, preferred_element_type=jnp.float32)

    def add_own(side):
        @pl.loop(0, PIECES // GROUP)
        def _(j):
            part = weigh(side, low[1 - side, pl.ds(j * chunk, chunk), :], j, True)

            @pl.when(j == 0)
            def _():
                total[side] = part

            @pl.when(j > 0)
            def _():
                total[side] += part

    def add_near(side, j):
        for i in range(GROUP):
            near_copy(low.at[0], side, j * GROUP + i).wait_recv()
        total[side] += weigh(side, near[side, pl.ds(j * chunk, chunk), :], j, False)

    def add_far(side, j):
        @pl.loop(j * GROUP, (j + 1) * GROUP)
        def _(i):
            far_copy(side, i, after).wait_recv()

            @pl.when(core == 1 - side)
            def _():
                near_copy(far.at[side], side, i).start()

        total[side] += weigh(side, far[side, pl.ds(j * chunk, chunk), :], j, False)

    def pass_on(first, last):
        @pl.when(middle)
        def _():
            @pl.loop(first, last)
            def _(j):
                @pl.when(relayed(j))
                def _():
                    relay_copy(j).wait_recv()

                    @pl.when(jnp.logical_not(bent))
                    def _():
                        onward_copy(j).start()

                    @pl.when(bent)
                    def _():
                        bent_copy(relay, pass_send.at[j], j).start()

    half = PIECES // 2
    pass_on(0, 1)
    add_own(0)

    @pl.when(waits)
    def _():
        pl.semaphore_wait(go_sem, 1)
        pl.loop(0, PIECES)(send_across)

        @pl.loop(AHEAD, PIECES)
        def _(j):
            send_along(1 - passing, j)

    pass_on(1, half)
    add_own(1)
    pass_on(half, half + 1)

    @pl.loop(0, PIECES // GROUP)
    def _(j):
        add_near(1 - core, j)

    pass_on(half + 1, PIECES)

    @pl.loop(0, PIECES)
    def _(j):
        @pl.when(bent_here(j))
        def _():
            bent_copy(low.at[0], bend_send.at[j], j).wait_recv()
            last_copy(j).start()

    lead = jnp.where(x == 0, 1, 0)

    @pl.loop(0, PIECES // GROUP)
    def _(j):
        add_far(lead, j)
        add_far(1 - lead, j)
        add_near(core, j)

    for side, out in enumerate((image_out, text_out)):

        @pl.loop(0, PIECES)
        def _(j):
            span = pl.ds(j * size, size)
            inv = inverse[side, span, :]
            unit = raw[side, span, :].astype(jnp.float32) * inv
            grad = total[side, span, :]
            along = jnp.sum(unit * grad, axis=-1, keepdims=True)
            out[span, :] = ((grad - unit * along) * inv).astype(jnp.bfloat16)

    @pl.loop(0, PIECES)
    def _(j):
        for side in range(2):
            far_copy(side, j, after).wait_send()
            near_copy(low.at[0], side, j).wait_send()

        @pl.when(jnp.logical_and(middle, relayed(j)))
        def _():
            onward_copy(j).wait_send()

        @pl.when(bent_here(j))
        def _():
            last_copy(j).wait_send()


def on_device(images, texts, log_scale, bias):
    rows, width = images.shape
    n = lax.axis_size("gx") * lax.axis_size("gy")
    block = (2, rows, width)
    dma = pltpu.SemaphoreType.DMA
    return pl.pallas_call(
        functools.partial(kernel, n),
        out_shape=[jax.ShapeDtypeStruct((rows, width), jnp.bfloat16)] * 2,
        in_specs=[pl.BlockSpec(memory_space=pltpu.SMEM)] * 2 + [pl.BlockSpec(memory_space=pltpu.HBM)] * 2,
        out_specs=[pl.BlockSpec(memory_space=pltpu.VMEM)] * 2,
        scratch_shapes=[
            pltpu.VMEM(block, jnp.bfloat16),
            pltpu.VMEM(block, jnp.bfloat16),
            pltpu.VMEM((2, rows, 1), jnp.float32),
            pltpu.VMEM(block, jnp.float32),
            pltpu.VMEM(block, jnp.bfloat16),
            pltpu.VMEM(block, jnp.bfloat16),
            pltpu.VMEM((rows, width), jnp.bfloat16),
            pltpu.VMEM((rows, width), jnp.bfloat16),
            dma((2, PIECES // GROUP)),
            dma((2, PIECES)),
            dma((2, PIECES)),
            dma((2, PIECES)),
            dma((2, PIECES)),
            dma((PIECES,)),
            dma((PIECES,)),
            dma((PIECES,)),
            dma((PIECES,)),
            pltpu.SemaphoreType.REGULAR,
        ],
        compiler_params=pltpu.CompilerParams(
            collective_id=0, has_side_effects=True, vmem_limit_bytes=51 * 1024 * 1024
        ),
        cost_estimate=pl.CostEstimate(
            flops=24 * rows * rows * width, bytes_accessed=8 * rows * width, transcendentals=6 * rows * rows
        ),
        name="contrast",
    )(log_scale, bias, images, texts)


def solution(mesh):
    return jax.shard_map(
        on_device,
        mesh=mesh,
        in_specs=(P(("gx", "gy"), None), P(("gx", "gy"), None), P(), P()),
        out_specs=(P(("gx", "gy"), None), P(("gx", "gy"), None)),
        check_vma=False,
    )
```

time: 70.7 us -> 62.8 us (0.89)
  the two profiles are of different devices: /device:TPU:128 before, /device:TPU:3 now
where the time goes in v3:
time: 62.8 us; the launch traced here: 62.7 us
  Pallas kernels  58.7 us (93%)
  local copies, waits for them, and re-layouts  2.03 us (3%)
  between operations  1.93 us (3%)
    pallas_call x1, Pallas kernels, on_device(): pl.pallas_call(functools.partial(kernel, n), out_shape=[jax.ShapeDtypeStr...  58.7 us
    unnamed x2, local copies, waits for them, and re-layouts  2.03 us

profile of v3, /device:TPU:3, one launch (start us, length us, event | category | flops | bytes accessed | tf_op | source)
XLA Modules:
  0.0 62.7 jit_solution(5202914598141594319)
XLA Ops:
  1.9 58.7 %contrast.1 = (bf16[512,1152]{1,0:T(8,128)(2,1)S(1)}, bf16[512,1152]{1,0:T(8,128)(2,1)S(1)}) custom-call(f32[1]{0:T(128)S(6)} %copy.8.scale_ref, f32[1]{0:T(128)S(6)} %copy.9.bias_ref, bf16[512,1152]{1,0:T(8,128)(2,1)} %images_ref.1, bf16[512,1152]{1,0:T(8,128)(2,1)} %texts_ref.1), custom_call_target="tpu_custom_call" | custom-call | flops 7247757312 | bytes 4718592 | tf_op jit(solution)/shard_map/contrast/pallas_call | solution.py:365
  60.6 1.0 %copy.10 = bf16[512,1152]{1,0:T(8,128)(2,1)} copy(bf16[512,1152]{1,0:T(8,128)(2,1)S(1)} %get-tuple-element.4) | data formatting | bytes 2359296
  61.7 1.0 %copy.11 = bf16[512,1152]{1,0:T(8,128)(2,1)} copy(bf16[512,1152]{1,0:T(8,128)(2,1)S(1)} %get-tuple-element.5) | data formatting | bytes 2359296

commit v4 on v3

--- a/solution.py
+++ b/solution.py
@@ -11,8 +11,7 @@
 MESH = pl.DeviceIdType.MESH
 PIECES = 8
 GROUP = 4
-RELAYED = 2
-AHEAD = 4
+CHUNKS = PIECES // GROUP
 
 
 def kernel(
@@ -94,92 +93,60 @@
         def _():
             load(images_ref, index, j // GROUP).wait()
 
-    def far_copy(side, j, partner):
-        span = pl.ds(j * size, size)
+    def rows_of(j, count=1):
+        return pl.ds(j * size, count * size)
+
+    def remote(source, target, send_sem, recv_sem, partner):
         return pltpu.make_async_remote_copy(
-            src_ref=low.at[1 - side, span],
-            dst_ref=far.at[side, span],
-            send_sem=far_send.at[side, j],
-            recv_sem=far_recv.at[side, j],
+            src_ref=source,
+            dst_ref=target,
+            send_sem=send_sem,
+            recv_sem=recv_sem,
             device_id=partner,
             device_id_type=MESH,
         )
 
+    def far_copy(side, j, count, partner):
+        span, c = rows_of(j, count), j // GROUP
+        return remote(low.at[1 - side, span], far.at[side, span], far_send.at[side, c], far_recv.at[side, c], partner)
+
+    def near_copy(source, side, c):
+        span = rows_of(c * GROUP, GROUP)
+        return remote(source.at[span], near.at[side, span], near_send.at[side, c], near_recv.at[side, c], sibling)
+
     def relay_copy(j):
-        span = pl.ds(j * size, size)
-        return pltpu.make_async_remote_copy(
-            src_ref=low.at[1 - passing, span],
-            dst_ref=relay.at[span],
-            send_sem=far_send.at[passing, j],
-            recv_sem=pass_recv.at[j],
-            device_id=helper,
-            device_id_type=MESH,
-        )
-
-    def onward_copy(j):
-        span = pl.ds(j * size, size)
-        return pltpu.make_async_remote_copy(
-            src_ref=relay.at[span],
-            dst_ref=far.at[passing, span],
-            send_sem=pass_send.at[j],
-            recv_sem=far_recv.at[passing, j],
-            device_id=onward,
-            device_id_type=MESH,
-        )
+        span = rows_of(j)
+        return remote(low.at[1 - passing, span], relay.at[span], far_send.at[passing, j // GROUP], pass_recv.at[j], helper)
+
+    def onward_copy(j, count=1):
+        span = rows_of(j, count)
+        return remote(relay.at[span], far.at[passing, span], pass_send, far_recv.at[passing, j // GROUP], onward)
 
     def bent_copy(source, send_sem, j):
-        span = pl.ds(j * size, size)
-        return pltpu.make_async_remote_copy(
-            src_ref=source.at[span],
-            dst_ref=bend.at[span],
-            send_sem=send_sem,
-            recv_sem=bend_recv.at[j],
-            device_id=corner,
-            device_id_type=MESH,
-        )
-
-    def last_copy(j):
-        span = pl.ds(j * size, size)
-        return pltpu.make_async_remote_copy(
-            src_ref=bend.at[span],
-            dst_ref=far.at[passing, span],
-            send_sem=bend_send.at[j],
-            recv_sem=far_recv.at[passing, j],
-            device_id=bent_to,
-            device_id_type=MESH,
-        )
-
-    def near_copy(source, side, j):
-        span = pl.ds(j * size, size)
-        return pltpu.make_async_remote_copy(
-            src_ref=source.at[span],
-            dst_ref=near.at[side, span],
-            send_sem=near_send.at[side, j],
-            recv_sem=near_recv.at[side, j],
-            device_id=sibling,
-            device_id_type=MESH,
-        )
+        span = rows_of(j)
+        return remote(source.at[span], bend.at[span], send_sem, bend_recv.at[j], corner)
+
+    def last_copy(j, count=1):
+        span = rows_of(j, count)
+        return remote(bend.at[span], far.at[passing, span], bend_send, far_recv.at[passing, j // GROUP], bent_to)
 
     def relayed(j):
-        return lax.rem(j, GROUP) < RELAYED
+        return lax.rem(j, GROUP) < GROUP // 2
 
     def send_across(j):
+        straight = jnp.logical_not(relayed(j))
+
         @pl.when(relayed(j))
         def _():
             relay_copy(j).start()
 
-        straight = jnp.logical_not(relayed(j))
-
         @pl.when(jnp.logical_and(straight, jnp.logical_not(bent)))
         def _():
-            far_copy(passing, j, across).start()
+            far_copy(passing, j, 1, across).start()
 
         @pl.when(jnp.logical_and(straight, bent))
         def _():
-            bent_copy(low.at[1 - passing], far_send.at[passing, j], j).start()
-
-    def bent_here(j):
-        return jnp.logical_and(bends, relayed(j) == middle)
+            bent_copy(low.at[1 - passing], far_send.at[passing, j // GROUP], j).start()
 
     def normalize(index, j):
         span = pl.ds(j * size, size)
@@ -188,12 +155,12 @@
         inverse[index, span, :] = inv
         low[index, span, :] = (values * inv).astype(jnp.bfloat16)
 
-    def send_along(side, j):
+    def send_along(side, j, count):
         for fixed, partner in enumerate((after, before)):
 
             @pl.when(side == fixed)
             def _():
-                far_copy(fixed, j, partner).start()
+                far_copy(fixed, j, count, partner).start()
 
     def enter(j):
         @pl.when(j == 0)
@@ -214,20 +181,21 @@
         def _():
             send_across(j)
 
-        @pl.when(jnp.logical_or(middle, jnp.logical_and(waits, j < AHEAD)))
-        def _():
-            send_along(1 - first, j)
+        @pl.when(jnp.logical_and(lax.rem(j, 2) == 1, jnp.logical_or(middle, jnp.logical_and(waits, j < GROUP))))
+        def _():
+            send_along(1 - first, j - 1, 2)
 
     @pl.loop(0, PIECES)
     def _(j):
         wait_load(1 - first, j)
         normalize(1 - first, j)
 
-        @pl.when(jnp.logical_or(middle, opens))
-        def _():
-            send_along(first, j)
-
-        near_copy(low.at[1 - core], core, j).start()
+        @pl.when(jnp.logical_and(lax.rem(j, 2) == 1, jnp.logical_or(middle, opens)))
+        def _():
+            send_along(first, j - 1, 2)
+
+    for c in range(CHUNKS):
+        near_copy(low.at[1 - core], core, c).start()
 
     scale = jnp.exp(jnp.full((1, chunk), scale_ref[0], jnp.float32))
     offset = bias_ref[0]
@@ -248,7 +216,7 @@
         return jnp.dot(coef, other, preferred_element_type=jnp.float32)
 
     def add_own(side):
-        @pl.loop(0, PIECES // GROUP)
+        @pl.loop(0, CHUNKS)
         def _(j):
             part = weigh(side, low[1 - side, pl.ds(j * chunk, chunk), :], j, True)
 
@@ -260,76 +228,64 @@
             def _():
                 total[side] += part
 
-    def add_near(side, j):
-        for i in range(GROUP):
-            near_copy(low.at[0], side, j * GROUP + i).wait_recv()
-        total[side] += weigh(side, near[side, pl.ds(j * chunk, chunk), :], j, False)
-
-    def add_far(side, j):
-        @pl.loop(j * GROUP, (j + 1) * GROUP)
-        def _(i):
-            far_copy(side, i, after).wait_recv()
-
-            @pl.when(core == 1 - side)
-            def _():
-                near_copy(far.at[side], side, i).start()
-
-        total[side] += weigh(side, far[side, pl.ds(j * chunk, chunk), :], j, False)
-
-    def pass_on(first, last):
+    def add_near(side, c):
+        near_copy(low.at[0], side, c).wait_recv()
+        total[side] += weigh(side, near[side, rows_of(c * GROUP, GROUP), :], c, False)
+
+    def add_far(c):
+        j = c * GROUP
+        far_copy(1 - core, j, GROUP, after).wait_recv()
+        near_copy(far.at[1 - core], 1 - core, c).start()
+        far_copy(core, j, GROUP, after).wait_recv()
+        for side in range(2):
+            total[side] += weigh(side, far[side, rows_of(j, GROUP), :], c, False)
+        add_near(core, c)
+
+    def pass_on(i):
         @pl.when(middle)
         def _():
-            @pl.loop(first, last)
-            def _(j):
-                @pl.when(relayed(j))
-                def _():
-                    relay_copy(j).wait_recv()
-
-                    @pl.when(jnp.logical_not(bent))
-                    def _():
-                        onward_copy(j).start()
-
-                    @pl.when(bent)
-                    def _():
-                        bent_copy(relay, pass_send.at[j], j).start()
-
-    half = PIECES // 2
-    pass_on(0, 1)
+            j = i // 2 * GROUP + i % 2
+            relay_copy(j).wait_recv()
+
+            @pl.when(jnp.logical_not(bent))
+            def _():
+                onward_copy(j).start()
+
+            @pl.when(bent)
+            def _():
+                bent_copy(relay, pass_send, j).start()
+
+    pass_on(0)
     add_own(0)
 
     @pl.when(waits)
     def _():
         pl.semaphore_wait(go_sem, 1)
         pl.loop(0, PIECES)(send_across)
-
-        @pl.loop(AHEAD, PIECES)
-        def _(j):
-            send_along(1 - passing, j)
-
-    pass_on(1, half)
+        send_along(1 - passing, GROUP, GROUP)
+
+    pass_on(1)
     add_own(1)
-    pass_on(half, half + 1)
-
-    @pl.loop(0, PIECES // GROUP)
-    def _(j):
-        add_near(1 - core, j)
-
-    pass_on(half + 1, PIECES)
-
-    @pl.loop(0, PIECES)
-    def _(j):
-        @pl.when(bent_here(j))
-        def _():
-            bent_copy(low.at[0], bend_send.at[j], j).wait_recv()
-            last_copy(j).start()
-
-    lead = jnp.where(x == 0, 1, 0)
-
-    @pl.loop(0, PIECES // GROUP)
-    def _(j):
-        add_far(lead, j)
-        add_far(1 - lead, j)
-        add_near(core, j)
+    pass_on(2)
+
+    @pl.loop(0, CHUNKS)
+    def _(c):
+        add_near(1 - core, c)
+
+    pass_on(3)
+
+    @pl.loop(0, CHUNKS)
+    def _(c):
+        add_far(c)
+
+        @pl.when(jnp.logical_and(bends, c == 0))
+        def _():
+            @pl.loop(0, PIECES)
+            def _(j):
+                @pl.when(relayed(j) == middle)
+                def _():
+                    bent_copy(relay, bend_send, j).wait_recv()
+                    last_copy(j).start()
 
     for side, out in enumerate((image_out, text_out)):
 
@@ -342,19 +298,18 @@
             along = jnp.sum(unit * grad, axis=-1, keepdims=True)
             out[span, :] = ((grad - unit * along) * inv).astype(jnp.bfloat16)
 
-    @pl.loop(0, PIECES)
-    def _(j):
-        for side in range(2):
-            far_copy(side, j, after).wait_send()
-            near_copy(low.at[0], side, j).wait_send()
-
-        @pl.when(jnp.logical_and(middle, relayed(j)))
-        def _():
-            onward_copy(j).wait_send()
-
-        @pl.when(bent_here(j))
-        def _():
-            last_copy(j).wait_send()
+    for side in range(2):
+        for c in range(CHUNKS):
+            far_copy(side, c * GROUP, GROUP, after).wait_send()
+            near_copy(low.at[0], side, c).wait_send()
+
+    @pl.when(middle)
+    def _():
+        onward_copy(0, GROUP).wait_send()
+
+    @pl.when(bends)
+    def _():
+        last_copy(0, GROUP).wait_send()
 
 
 def on_device(images, texts, log_scale, bias):
@@ -376,14 +331,14 @@
             pltpu.VMEM(block, jnp.bfloat16),
             pltpu.VMEM((rows, width), jnp.bfloat16),
             pltpu.VMEM((rows, width), jnp.bfloat16),
-            dma((2, PIECES // GROUP)),
-            dma((2, PIECES)),
-            dma((2, PIECES)),
-            dma((2, PIECES)),
-            dma((2, PIECES)),
+            dma((2, CHUNKS)),
+            dma((2, CHUNKS)),
+            dma((2, CHUNKS)),
+            dma((2, CHUNKS)),
+            dma((2, CHUNKS)),
+            dma,
             dma((PIECES,)),
-            dma((PIECES,)),
-            dma((PIECES,)),
+            dma,
             dma((PIECES,)),
             pltpu.SemaphoreType.REGULAR,
         ],

time: 62.8 us -> 60.8 us (0.968)
  the two profiles are of different devices: /device:TPU:3 before, /device:TPU:128 now
where the time goes in v4:
time: 60.8 us; the launch traced here: 60.7 us
  Pallas kernels  56.7 us (93%)
  local copies, waits for them, and re-layouts  2.03 us (3%)
  between operations  1.93 us (3%)
    pallas_call x1, Pallas kernels, on_device(): pl.pallas_call(functools.partial(kernel, n), out_shape=[jax.ShapeDtypeStr...  56.7 us
    unnamed x2, local copies, waits for them, and re-layouts  2.03 us

profile of v4, /device:TPU:128, one launch (start us, length us, event | category | flops | bytes accessed | tf_op | source)
XLA Modules:
  0.0 60.7 jit_solution(3500805494636604872)
XLA Ops:
  1.9 56.7 %contrast.1 = (bf16[512,1152]{1,0:T(8,128)(2,1)S(1)}, bf16[512,1152]{1,0:T(8,128)(2,1)S(1)}) custom-call(f32[1]{0:T(128)S(6)} %copy.8.scale_ref, f32[1]{0:T(128)S(6)} %copy.9.bias_ref, bf16[512,1152]{1,0:T(8,128)(2,1)} %images_ref.1, bf16[512,1152]{1,0:T(8,128)(2,1)} %texts_ref.1), custom_call_target="tpu_custom_call" | custom-call | flops 7247757312 | bytes 4718592 | tf_op jit(solution)/shard_map/contrast/pallas_call | solution.py:320
  58.7 1.0 %copy.10 = bf16[512,1152]{1,0:T(8,128)(2,1)} copy(bf16[512,1152]{1,0:T(8,128)(2,1)S(1)} %get-tuple-element.4) | data formatting | bytes 2359296
  59.7 1.0 %copy.11 = bf16[512,1152]{1,0:T(8,128)(2,1)} copy(bf16[512,1152]{1,0:T(8,128)(2,1)S(1)} %get-tuple-element.5) | data formatting | bytes 2359296
